TPU v7x, 32 devices: a whole 2x2x4 slice. The times are simulated.
32 devices in a mesh: groups: 2 (over y), tm: 8 (over z, x), head: 2 (over core).
Axes of the slice: x: 2, y: 2, z: 4, core: 2. Of those that a mesh axis runs over, the one named last changes fastest.
Arguments:
- queries: bfloat16 [1536, 2560], P(('groups', 'tm'), 'head'), parts along dimension 0, may hold values from -1000 to 1000
- keys: bfloat16 [1536, 2560], P(('groups', 'tm'), 'head'), parts along dimension 0, may hold values from -1000 to 1000
- values: bfloat16 [1536, 2560], P(('groups', 'tm'), 'head'), parts along dimension 0, may hold values from -6 to 6
- q_gain: float32 [2560], P('head'), may hold values from 1 to 2
- k_gain: float32 [2560], P('head'), may hold values from 1 to 2
- frames: int32 [16], P(('groups', 'tm')), parts along dimension 0, may hold values from 1 to 3
- flags: int32 [16, 2], P(('groups', 'tm')), parts along dimension 0, may hold values 0 or 1
Outputs:
- attended: bfloat16 [1536, 2560], P(('groups', 'tm'), 'head'), parts along dimension 0
There are 2 independent parts, one for each index of `groups`. A program takes and returns all parts, laid end to end along the dimension named above; an argument that names none is the same for every part. Nothing has to cross between parts.
All inputs are finite; a program needn't handle non-finite values. No bound on the sum of `flags` on one device may be relied on, other than what follows from the above.
Results may differ from a plain program's by a relative error of at most 0.011.
Values may be sent and summed in bfloat16 or wider, within the bound.
A program may use at most 128 MiB of HBM per device.

v0:
```python
from functools import reduce
import math

import jax
import jax.numpy as jnp
from jax import lax
from jax.sharding import PartitionSpec as P

HD = 128
FT = 32


EPSILON = 1e-06


def passed_along(value, axis, steps):
    count = lax.axis_size(axis)
    first, last = (max(0, -steps), min(count, count - steps))
    return lax.ppermute(value, axis, [(source, source + steps) for source in range(first, last)])


def spread(value, axis, source):
    kept = jnp.where(lax.axis_index(axis) == source, value, 0).astype(value.dtype)
    return lax.psum(kept, axis)


def slide_rows(buffer, offset_rows, window_len):
    filler = jnp.zeros((window_len,) + buffer.shape[1:], buffer.dtype)
    return lax.dynamic_slice_in_dim(
        jnp.concatenate([buffer, filler], 0), offset_rows, window_len, 0
    )


def append_window(earlier, later):
    window_len = later[2].shape[0]
    later_count = jnp.sum(later[2].astype(jnp.float32)).astype(jnp.int32)
    from_later = jnp.arange(window_len, dtype=jnp.int32) >= window_len - later_count
    merged = []
    for previous, incoming in zip(earlier, later):
        shifted = slide_rows(previous, later_count, window_len)
        choose_mask = from_later.reshape((window_len,) + (1,) * (incoming.ndim - 1))
        merged.append(jnp.where(choose_mask, incoming, shifted))
    return tuple(merged)


def local(queries, keys, values, q_gain, k_gain, frames, flags):
    row_count, col_count = queries.shape
    head_count = col_count // HD
    full_width = col_count * lax.axis_size("head")
    q_wide = queries.astype(jnp.float32)
    k_wide = keys.astype(jnp.float32)
    q_energy, k_energy = lax.psum(
        (jnp.sum(q_wide * q_wide, axis=1), jnp.sum(k_wide * k_wide, axis=1)), "head"
    )
    q_norm = (q_wide * lax.rsqrt(q_energy / full_width + EPSILON)[:, None] * q_gain).astype(
        jnp.bfloat16
    )
    k_norm = (k_wide * lax.rsqrt(k_energy / full_width + EPSILON)[:, None] * k_gain).astype(
        jnp.bfloat16
    )
    valid_rows = frames[0] * FT
    window_len = 2 * FT

    def tail_rows(source):
        leading = jnp.zeros((window_len, col_count), jnp.bfloat16)
        return slide_rows(jnp.concatenate([leading, source], 0), valid_rows, window_len)

    own_flags = (jnp.arange(window_len, dtype=jnp.int32) >= window_len - valid_rows).astype(
        jnp.bfloat16
    )
    own_window = (tail_rows(k_norm), tail_rows(values), own_flags)
    from_last = passed_along((own_window[0], own_window[1], own_window[2]), "tm", 1)
    from_earlier = passed_along((own_window[0], own_window[1], own_window[2]), "tm", 2)
    window_keys, window_values, window_flags = append_window(from_earlier, from_last)
    sink_keys, sink_values = (spread(k_norm[:FT], "tm", 0), spread(values[:FT], "tm", 0))
    scaling = 1.0 / math.sqrt(HD)
    q_heads = q_norm.reshape(row_count, head_count, HD)
    slot_index = jnp.arange(row_count, dtype=jnp.int32)
    live_keys = slot_index < valid_rows
    use_sink = flags[0, 0] > 0
    use_window = flags[0, 1] > 0
    key_groups = (
        (k_norm, values, live_keys),
        (window_keys, window_values, (window_flags > 0) & use_window),
        (sink_keys, sink_values, jnp.full((sink_keys.shape[0],), use_sink)),
    )

    def score_block(key_rows, allowed):
        k_heads = key_rows.reshape(key_rows.shape[0], head_count, HD)
        products = (
            jnp.einsum("qhd,khd->hqk", q_heads, k_heads, preferred_element_type=jnp.float32)
            * scaling
        )
        return jnp.where(allowed[None, None, :], products, -jnp.inf)

    logits = [score_block(key_rows, allowed) for key_rows, value_rows, allowed in key_groups]
    highest = reduce(
        jnp.maximum, [jnp.max(block_scores, axis=2, keepdims=True) for block_scores in logits]
    )
    denominator = jnp.zeros((head_count, row_count), jnp.float32)
    blended = jnp.zeros((row_count, head_count, HD), jnp.float32)
    for block_scores, group in zip(logits, key_groups):
        weight = jnp.exp(block_scores - highest).astype(jnp.bfloat16)
        denominator = denominator + jnp.sum(weight, axis=2, dtype=jnp.float32)
        value_heads = group[1].reshape(group[1].shape[0], head_count, HD)
        blended = blended + jnp.einsum(
            "hqk,khd->qhd", weight, value_heads, preferred_element_type=jnp.float32
        )
    blended = blended / jnp.transpose(denominator)[:, :, None]
    blended = jnp.where(live_keys[:, None, None], blended, 0.0)
    return blended.reshape(row_count, col_count).astype(jnp.bfloat16)


def solution(mesh):
    placed = (
        P(("groups", "tm"), "head"),
        P(("groups", "tm"), "head"),
        P(("groups", "tm"), "head"),
        P("head"),
        P("head"),
        P(("groups", "tm")),
        P(("groups", "tm"), None),
    )
    return jax.shard_map(
        local, mesh=mesh, in_specs=placed, out_specs=P(("groups", "tm"), "head"), check_vma=False
    )
```

profile of v0, /device:TPU:0, one launch (start us, length us, event | category | flops | bytes accessed | tf_op | source)
XLA Modules:
  0.0 110.7 jit_solution(5486374469623921674)
XLA Ops:
  7.2 4.9 %collective-permute-start.1 = (bf16[64]{0:T(256)(128)(2,1)S(1)}, bf16[64]{0:T(256)(128)(2,1)S(1)}, u32[]{:S(2)}, u32[]{:S(2)}) collective-permute-start(bf16[64]{0:T(256)(128)(2,1)S(1)} %compare_convert_fusion), channel_id=1, source_target_pairs={{0,4},{2,6},{4,8},{6,10},{8,12},{10,14},{1,5},{3,7},{5,9},{7,11},{... | collective-permute-start | bytes 392 | tf_op jit(solution)/shard_map/ppermute | solution.py:19
  12.2 3.4 %collective-permute-start = (bf16[64]{0:T(256)(128)(2,1)S(1)}, bf16[64]{0:T(256)(128)(2,1)S(1)}, u32[]{:S(2)}, u32[]{:S(2)}) collective-permute-start(bf16[64]{0:T(256)(128)(2,1)S(1)} %compare_convert_fusion), channel_id=1, source_target_pairs={{0,2},{2,4},{4,6},{6,8},{8,10},{10,12},{12,14},{1,3},{3,5},{5,7},{... | collective-permute-start | bytes 392 | tf_op jit(solution)/shard_map/ppermute | solution.py:19
  15.6 1.1 fusion.7
  16.9 2.5 %all-reduce.3 = (f32[96]{0:T(128)S(1)}, f32[96]{0:T(128)S(1)}) all-reduce(f32[96]{0:T(128)S(1)} %fusion.7, f32[96]{0:T(128)S(1)} %fusion.10), channel_id=1, replica_groups=mesh['groups'=2,'tm'=8,'head'=2] {'head'}, use_global_device_ids=true, to_apply=%region_1.0 | all-reduce | flops 192 | bytes 1536 | tf_op jit(solution)/shard_map/psum | solution.py:52
  19.5 0.8 copy-done
  20.5 3.5 %collective-permute-start.4 = (bf16[64,1280]{1,0:T(8,128)(2,1)S(1)}, bf16[64,1280]{1,0:T(8,128)(2,1)S(1)}, u32[]{:S(2)}, u32[]{:S(2)}) collective-permute-start(bf16[64,1280]{1,0:T(8,128)(2,1)S(1)} %get-tuple-element.9), channel_id=1, source_target_pairs={{0,2},{2,4},{4,6},{6,8},{8,10},{10,12},{12,14},{1,3},{3,5},{5,7},{... | collective-permute-start | bytes 491528 | tf_op jit(solution)/shard_map/ppermute | solution.py:19
  23.9 3.5 %collective-permute-start.5 = (bf16[64,1280]{1,0:T(8,128)(2,1)S(1)}, bf16[64,1280]{1,0:T(8,128)(2,1)S(1)}, u32[]{:S(2)}, u32[]{:S(2)}) collective-permute-start(bf16[64,1280]{1,0:T(8,128)(2,1)S(1)} %get-tuple-element.9), channel_id=1, source_target_pairs={{0,4},{2,6},{4,8},{6,10},{8,12},{10,14},{1,5},{3,7},{5,9},{7,11},{... | collective-permute-start | bytes 491528 | tf_op jit(solution)/shard_map/ppermute | solution.py:19
  27.4 3.4 %collective-permute-start.2 = (bf16[64,1280]{1,0:T(8,128)(2,1)S(1)}, bf16[64,1280]{1,0:T(8,128)(2,1)S(1)}, u32[]{:S(2)}, u32[]{:S(2)}) collective-permute-start(bf16[64,1280]{1,0:T(8,128)(2,1)S(1)} %get-tuple-element.10), channel_id=1, source_target_pairs={{0,2},{2,4},{4,6},{6,8},{8,10},{10,12},{12,14},{1,3},{3,5},{5,7},{... | collective-permute-start | bytes 491528 | tf_op jit(solution)/shard_map/ppermute | solution.py:19
  30.8 0.6 copy_bitcast_fusion
  31.5 0.7 copy_bitcast_fusion.1
  32.7 0.4 copy-done.5
  33.1 0.6 fusion.26
  34.7 0.3 fusion.28
  35.7 1.9 %collective-permute-start.3 = (bf16[64,1280]{1,0:T(8,128)(2,1)S(1)}, bf16[64,1280]{1,0:T(8,128)(2,1)S(1)}, u32[]{:S(2)}, u32[]{:S(2)}) collective-permute-start(bf16[64,1280]{1,0:T(8,128)(2,1)S(1)} %get-tuple-element.10), channel_id=1, source_target_pairs={{0,4},{2,6},{4,8},{6,10},{8,12},{10,14},{1,5},{3,7},{5,9},{7,11},{... | collective-permute-start | bytes 491528 | tf_op jit(solution)/shard_map/ppermute | solution.py:19
  37.6 0.7 convert_reduce_fusion.3
  39.0 60.2 %all-reduce.7.cloned.1.call-done = (bf16[32,10,128]{2,0,1:T(8,128)(2,1)}, bf16[32,10,128]{2,0,1:T(8,128)(2,1)}) async-done(((bf16[32,10,128]{2,0,1:T(8,128)(2,1)}, bf16[32,10,128]{2,0,1:T(8,128)(2,1)}), (bf16[32,10,128]{2,0,1:T(8,128)(2,1)}, bf16[32,10,128]{2,0,1:T(8,128)(2,1)})) %all-reduce.7.cloned.1.call-update) | async-done | bytes 163856 | tf_op jit(solution)/shard_map/psum | solution.py:24
  99.2 1.1 fusion.27
  100.5 0.2 select_reduce_fusion
  101.1 0.4 convolution_bitcast_fusion.2
  101.5 0.4 fusion.1
  101.9 0.5 copy-done.6
  102.4 0.3 fusion.5
  102.7 0.2 copy.29
  102.9 0.9 copy.30
  (38 shorter events, 1.9 us)
Async XLA Ops:
  6.5 10.2 %copy-start.1 = (bf16[96,1280]{1,0:T(8,128)(2,1)S(1)}, bf16[96,1280]{1,0:T(8,128)(2,1)}, u32[]{:S(2)}) copy-start(bf16[96,1280]{1,0:T(8,128)(2,1)} %param.8) | copy-start | bytes 737284
  6.5 92.7 %all-reduce.7.cloned.1.call-start = ((), (), s32[]{:S(2)}) async-start(), calls=%async_computation | async-start | bytes 327680 | tf_op jit(solution)/shard_map/psum | solution.py:24
  7.2 31.6 %collective-permute-start.1 = (bf16[64]{0:T(256)(128)(2,1)S(1)}, bf16[64]{0:T(256)(128)(2,1)S(1)}, u32[]{:S(2)}, u32[]{:S(2)}) collective-permute-start(bf16[64]{0:T(256)(128)(2,1)S(1)} %compare_convert_fusion), channel_id=1, source_target_pairs={{0,4},{2,6},{4,8},{6,10},{8,12},{10,14},{1,5},{3,7},{5,9},{7,11},{... | collective-permute-start | bytes 392 | tf_op jit(solution)/shard_map/ppermute | solution.py:19
  12.2 23.5 %collective-permute-start = (bf16[64]{0:T(256)(128)(2,1)S(1)}, bf16[64]{0:T(256)(128)(2,1)S(1)}, u32[]{:S(2)}, u32[]{:S(2)}) collective-permute-start(bf16[64]{0:T(256)(128)(2,1)S(1)} %compare_convert_fusion), channel_id=1, source_target_pairs={{0,2},{2,4},{4,6},{6,8},{8,10},{10,12},{12,14},{1,3},{3,5},{5,7},{... | collective-permute-start | bytes 392 | tf_op jit(solution)/shard_map/ppermute | solution.py:19
  16.8 2.5 %copy-start.3 = (f32[1280]{0:T(1024)S(1)}, f32[1280]{0:T(1024)}, u32[]{:S(2)}) copy-start(f32[1280]{0:T(1024)} %param.11) | copy-start | bytes 15364
  19.3 0.9 copy-start
  20.5 79.9 %collective-permute-start.4 = (bf16[64,1280]{1,0:T(8,128)(2,1)S(1)}, bf16[64,1280]{1,0:T(8,128)(2,1)S(1)}, u32[]{:S(2)}, u32[]{:S(2)}) collective-permute-start(bf16[64,1280]{1,0:T(8,128)(2,1)S(1)} %get-tuple-element.9), channel_id=1, source_target_pairs={{0,2},{2,4},{4,6},{6,8},{8,10},{10,12},{12,14},{1,3},{3,5},{5,7},{... | collective-permute-start | bytes 491528 | tf_op jit(solution)/shard_map/ppermute | solution.py:19
  23.9 76.4 %collective-permute-start.5 = (bf16[64,1280]{1,0:T(8,128)(2,1)S(1)}, bf16[64,1280]{1,0:T(8,128)(2,1)S(1)}, u32[]{:S(2)}, u32[]{:S(2)}) collective-permute-start(bf16[64,1280]{1,0:T(8,128)(2,1)S(1)} %get-tuple-element.9), channel_id=1, source_target_pairs={{0,4},{2,6},{4,8},{6,10},{8,12},{10,14},{1,5},{3,7},{5,9},{7,11},{... | collective-permute-start | bytes 491528 | tf_op jit(solution)/shard_map/ppermute | solution.py:19
  27.4 72.9 %collective-permute-start.2 = (bf16[64,1280]{1,0:T(8,128)(2,1)S(1)}, bf16[64,1280]{1,0:T(8,128)(2,1)S(1)}, u32[]{:S(2)}, u32[]{:S(2)}) collective-permute-start(bf16[64,1280]{1,0:T(8,128)(2,1)S(1)} %get-tuple-element.10), channel_id=1, source_target_pairs={{0,2},{2,4},{4,6},{6,8},{8,10},{10,12},{12,14},{1,3},{3,5},{5,7},{... | collective-permute-start | bytes 491528 | tf_op jit(solution)/shard_map/ppermute | solution.py:19
  32.4 0.7 copy-start.5
  32.4 1.3 %copy-start.2 = (bf16[96,1280]{1,0:T(8,128)(2,1)S(1)}, bf16[96,1280]{1,0:T(8,128)(2,1)}, u32[]{:S(2)}) copy-start(bf16[96,1280]{1,0:T(8,128)(2,1)} %param.7) | copy-start | bytes 737284
  32.4 1.3 %copy-start.4 = (f32[1280]{0:T(1024)S(1)}, f32[1280]{0:T(1024)}, u32[]{:S(2)}) copy-start(f32[1280]{0:T(1024)} %param.10) | copy-start | bytes 15364
  35.7 64.7 %collective-permute-start.3 = (bf16[64,1280]{1,0:T(8,128)(2,1)S(1)}, bf16[64,1280]{1,0:T(8,128)(2,1)S(1)}, u32[]{:S(2)}, u32[]{:S(2)}) collective-permute-start(bf16[64,1280]{1,0:T(8,128)(2,1)S(1)} %get-tuple-element.10), channel_id=1, source_target_pairs={{0,4},{2,6},{4,8},{6,10},{8,12},{10,14},{1,5},{3,7},{5,9},{7,11},{... | collective-permute-start | bytes 491528 | tf_op jit(solution)/shard_map/ppermute | solution.py:19
  101.5 0.9 copy-start.6
Sparse Core Ops, SparseCore 0:
  32.3 66.8 all-reduce.6
where the time goes:
time: 111 us
  waiting for transfers between devices  60.3 us (54%)
  starting transfers between devices  20.6 us (19%)
  between operations  16.3 us (15%)
  other arithmetic  4.21 us (4%)
  local copies, waits for them, and re-layouts  4.14 us (4%)
  matrix products  2.67 us (2%)
  blocking collectives  2.47 us (2%)
    psum x1, waiting for transfers between devices, spread(): return lax.psum(kept, axis)  60.2 us
    ppermute x6, starting transfers between devices, passed_along(): lax.ppermute(value, axis, [(source, source + steps) for source in range(f...  20.6 us
    psum x1, blocking collectives, local(): lax.psum((jnp.sum(q_wide * q_wide, axis=1), jnp.sum(k_wide * k_wide, axis...  2.47 us
  transfers between devices with their start and end apart: 7, of which 1 were waited for; matrix products, arithmetic and copies ran while one was open for 6% of the time, Pallas kernels for 0%

commit v1 on v0

v1 whole, which is shorter than its diff:
```python
import functools
import math

import jax
import jax.numpy as jnp
from jax import lax
from jax.experimental import pallas as pl
from jax.experimental.pallas import tpu as pltpu
from jax.sharding import PartitionSpec as P

HD = 128
FT = 32
EPSILON = 1e-06
MASKED = -1e30

ENERGY, COUNT, V_NEW, K_NEW, V_OLD, K_OLD, V_SINK, K_SINK = range(8)


def kernel(spans, heads_axis, q_hbm, k_hbm, v_hbm, q_gain, k_gain, frames, flags, out,
           q_raw, k_raw, q_norm, k_all, v_all, energy, energy_in, count, count_in,
           v_new, k_new, v_old, k_old, own_max, own_sum, own_out,
           local_sem, send_sem, recv_sem, hop_sem):
    rows, cols = q_hbm.shape
    heads = cols // HD
    window = 2 * FT
    older, newer, sink = rows, rows + FT, rows + window
    full_width = cols * heads_axis
    t = lax.axis_index("tm")
    side = lax.axis_index("head")
    even = t % 2 == 0

    def column(h):
        return pl.ds(h * HD, HD)

    def load(source, target, index):
        return pltpu.make_async_copy(source, target, local_sem.at[index])

    loads = [load(k_hbm, k_raw, 0), load(q_hbm, q_raw, 1), load(v_hbm, v_all.at[pl.ds(0, rows)], 2)]
    for copy in loads:
        copy.start()

    barrier = pltpu.get_barrier_semaphore()

    def greet(condition, **where):
        @pl.when(condition)
        def _():
            pl.semaphore_signal(barrier, inc=1, device_id=where, device_id_type=pl.DeviceIdType.MESH)

    for other in range(1, heads_axis):
        greet(side >= 0, head=lax.rem(side + other, heads_axis))
    partners = heads_axis - 1
    for step in (-2, -1, 1, 2):
        there = (t + step >= 0) & (t + step < spans)
        greet(there, tm=t + step)
        partners = partners + there.astype(jnp.int32)

    n = frames[0] * FT

    @pl.when(t == 0)
    def _():
        blank = jnp.zeros((window, cols), jnp.bfloat16)
        k_all[pl.ds(older, window)] = blank
        v_all[pl.ds(older, window)] = blank
        count_in[...] = jnp.zeros_like(count_in)

    count[...] = jnp.full(count.shape, n, jnp.int32)

    def remote(kind, source, target, sem=None, **where):
        return pltpu.make_async_remote_copy(
            src_ref=source, dst_ref=target,
            send_sem=send_sem.at[kind] if sem is None else sem, recv_sem=recv_sem.at[kind],
            device_id=where, device_id_type=pl.DeviceIdType.MESH)

    after = {"tm": jnp.minimum(t + 1, spans - 1)}
    before = {"tm": jnp.maximum(t - 1, 0)}
    hop = {"tm": jnp.minimum(t + 2, spans - 1)}
    has_after = t + 1 < spans
    has_hop = t + 2 < spans

    def squares(ref):
        total = jnp.zeros((rows, HD), jnp.float32)
        for h in range(heads):
            block = ref[:, column(h)].astype(jnp.float32)
            total = total + block * block
        return total

    loads[0].wait()
    energy[0] = squares(k_raw)
    loads[1].wait()
    energy[1] = squares(q_raw)

    pl.semaphore_wait(barrier, partners)
    share = remote(ENERGY, energy, energy_in, head=lax.rem(side + 1, heads_axis))
    share.start()

    loads[2].wait()

    def newest(source, target):
        for h in range(heads):
            a, b, c = (source[pl.ds(i * FT, FT), column(h)] for i in range(3))
            target[:, column(h)] = jnp.where(n >= 3 * FT, c, jnp.where(n >= 2 * FT, b, a))

    def second(source, target):
        for h in range(heads):
            a, b = (source[pl.ds(i * FT, FT), column(h)] for i in range(2))
            got = source[pl.ds(newer, FT), column(h)]
            target[:, column(h)] = jnp.where(n >= 3 * FT, b, jnp.where(n >= 2 * FT, a, got))

    counts = remote(COUNT, count, count_in, **after)
    sends = {
        V_NEW: remote(V_NEW, v_new, v_all.at[pl.ds(newer, FT)], **after),
        K_NEW: remote(K_NEW, k_new, k_all.at[pl.ds(newer, FT)], **after),
        V_OLD: remote(V_OLD, v_old, v_all.at[pl.ds(older, FT)], **after),
        K_OLD: remote(K_OLD, k_old, k_all.at[pl.ds(older, FT)], **after),
    }

    def sink_sends(kind, ref):
        at = ref.at[pl.ds(sink, FT)]
        along = remote(kind, at, at, sem=hop_sem.at[kind - V_SINK], **hop)
        across = remote(kind, at, at, **after)
        return along, across

    def sink_pass(kind, ref):
        along, across = sink_sends(kind, ref)

        @pl.when(even & has_hop)
        def _():
            along.start()

        @pl.when(even & has_after)
        def _():
            across.start()

    def sink_take(kind, ref):
        @pl.when(t > 0)
        def _():
            sink_sends(kind, ref)[1].wait_recv()

    @pl.when(t == 0)
    def _():
        v_all[pl.ds(sink, FT)] = v_all[pl.ds(0, FT)]
        sink_pass(V_SINK, v_all)

    newest(v_all, v_new)

    @pl.when(has_after)
    def _():
        sends[V_NEW].start()
        counts.start()

    share.wait()

    def level(index):
        total = jnp.sum(energy[index] + energy_in[index], axis=1, keepdims=True)
        return lax.rsqrt(total / full_width + EPSILON)

    k_level, q_level = level(0), level(1)
    for h in range(heads):
        k_all[pl.ds(0, rows), column(h)] = (
            k_raw[:, column(h)].astype(jnp.float32) * k_level * k_gain[:, column(h)]
        ).astype(jnp.bfloat16)

    @pl.when(t == 0)
    def _():
        k_all[pl.ds(sink, FT)] = k_all[pl.ds(0, FT)]
        sink_pass(K_SINK, k_all)

    newest(k_all, k_new)

    @pl.when(has_after)
    def _():
        sends[K_NEW].start()

    for h in range(heads):
        q_norm[:, column(h)] = (
            q_raw[:, column(h)].astype(jnp.float32) * q_level * q_gain[:, column(h)]
        ).astype(jnp.bfloat16)

    def received(kind):
        @pl.when(t > 0)
        def _():
            sends[kind].wait_recv()

    scaling = math.log2(math.e) / math.sqrt(HD)

    def scores(h, start, allowed):
        products = lax.dot_general(
            q_norm[:, column(h)], k_all[pl.ds(start, rows), column(h)],
            (((1,), (1,)), ((), ())), preferred_element_type=jnp.float32)
        return jnp.where(allowed, products * scaling, MASKED)

    def mix(weight, h, start):
        return jnp.dot(weight.astype(jnp.bfloat16), v_all[pl.ds(start, rows), column(h)],
                       preferred_element_type=jnp.float32)

    lane = lax.broadcasted_iota(jnp.int32, (1, rows), 1)
    live_keys = lane < n
    live_rows = lax.broadcasted_iota(jnp.int32, (rows, 1), 0) < n

    def own(h):
        s = scores(h, 0, live_keys)
        top = jnp.max(s, axis=1, keepdims=True)
        weight = jnp.exp2(s - top)
        own_max[h] = top
        own_sum[h] = jnp.sum(weight, axis=1, keepdims=True)
        own_out[:, column(h)] = mix(weight, h, 0)

    third = heads // 3
    received(V_NEW)
    second(v_all, v_old)

    @pl.when(has_after)
    def _():
        sends[V_OLD].start()

    for h in range(third):
        own(h)

    received(K_NEW)
    second(k_all, k_old)

    @pl.when(has_after)
    def _():
        sends[K_OLD].start()

    sink_take(V_SINK, v_all)

    @pl.when(t > 0)
    def _():
        sink_pass(V_SINK, v_all)

    for h in range(third, 2 * third):
        own(h)
    sink_take(K_SINK, k_all)

    @pl.when(t > 0)
    def _():
        sink_pass(K_SINK, k_all)

    for h in range(2 * third, heads):
        own(h)

    @pl.when(t > 0)
    def _():
        counts.wait_recv()

    received(V_OLD)
    received(K_OLD)

    use_sink = flags[0, 0]
    use_window = flags[0, 1]
    held = jnp.where(t >= 2, window, count_in[0:1, :rows])
    allowed = jnp.where(
        lane >= window, use_sink,
        use_window * jnp.where(lane >= FT, (held > 0).astype(jnp.int32),
                               (held >= window).astype(jnp.int32))) > 0

    for h in range(heads):
        s = scores(h, older, allowed)
        top = jnp.maximum(jnp.max(s, axis=1, keepdims=True), own_max[h])
        weight = jnp.exp2(s - top)
        keep = jnp.exp2(own_max[h] - top)
        denominator = jnp.sum(weight, axis=1, keepdims=True) + own_sum[h] * keep
        total = mix(weight, h, older) + own_out[:, column(h)] * keep
        out[:, column(h)] = jnp.where(live_rows, total / denominator, 0.0).astype(jnp.bfloat16)

    @pl.when(has_after)
    def _():
        counts.wait_send()
        for copy in sends.values():
            copy.wait_send()

    for kind, ref in ((V_SINK, v_all), (K_SINK, k_all)):
        along, across = sink_sends(kind, ref)

        @pl.when(even & has_hop)
        def _():
            along.wait_send()

        @pl.when(even & has_after)
        def _():
            across.wait_send()


def local(spans, heads_axis, queries, keys, values, q_gain, k_gain, frames, flags):
    rows, cols = queries.shape
    heads = cols // HD
    far = pl.BlockSpec(memory_space=pl.ANY)
    near = pl.BlockSpec(memory_space=pltpu.VMEM)
    scalar = pl.BlockSpec(memory_space=pltpu.SMEM)
    bf16, f32 = jnp.bfloat16, jnp.float32
    held = 2 * rows
    return pl.pallas_call(
        functools.partial(kernel, spans, heads_axis),
        out_shape=jax.ShapeDtypeStruct((rows, cols), bf16),
        in_specs=[far, far, far, near, near, scalar, scalar],
        out_specs=near,
        scratch_shapes=[
            pltpu.VMEM((rows, cols), bf16),
            pltpu.VMEM((rows, cols), bf16),
            pltpu.VMEM((rows, cols), bf16),
            pltpu.VMEM((held, cols), bf16),
            pltpu.VMEM((held, cols), bf16),
            pltpu.VMEM((2, rows, HD), f32),
            pltpu.VMEM((2, rows, HD), f32),
            pltpu.VMEM((8, HD), jnp.int32),
            pltpu.VMEM((8, HD), jnp.int32),
            pltpu.VMEM((FT, cols), bf16),
            pltpu.VMEM((FT, cols), bf16),
            pltpu.VMEM((FT, cols), bf16),
            pltpu.VMEM((FT, cols), bf16),
            pltpu.VMEM((heads, rows, 1), f32),
            pltpu.VMEM((heads, rows, 1), f32),
            pltpu.VMEM((rows, cols), f32),
            pltpu.SemaphoreType.DMA((3,)),
            pltpu.SemaphoreType.DMA((8,)),
            pltpu.SemaphoreType.DMA((8,)),
            pltpu.SemaphoreType.DMA((2,)),
        ],
        compiler_params=pltpu.CompilerParams(
            collective_id=0, has_side_effects=True, vmem_limit_bytes=32 * 2**20),
    )(queries, keys, values, q_gain.reshape(1, cols), k_gain.reshape(1, cols), frames, flags)


def solution(mesh):
    placed = (
        P(("groups", "tm"), "head"),
        P(("groups", "tm"), "head"),
        P(("groups", "tm"), "head"),
        P("head"),
        P("head"),
        P(("groups", "tm")),
        P(("groups", "tm"), None),
    )
    return jax.shard_map(
        functools.partial(local, mesh.shape["tm"], mesh.shape["head"]),
        mesh=mesh, in_specs=placed, out_specs=P(("groups", "tm"), "head"), check_vma=False
    )
```

time: 111 us -> 30 us (0.27)
  the two profiles are of different devices: /device:TPU:0 before, /device:TPU:26 now
where the time goes in v1:
time: 30 us; the launch traced here: 29.7 us
  Pallas kernels  24.2 us (81%)
  local copies, waits for them, and re-layouts  4.88 us (16%)
  between operations  0.69 us (2%)
    pallas_call x1, Pallas kernels, local(): pl.pallas_call(functools.partial(kernel, spans, heads_axis), out_shape=ja...  24.2 us
    unnamed x11, local copies, waits for them, and re-layouts  4.17 us
    reshape x1, local copies, waits for them, and re-layouts, local(): q_gain.reshape(1, cols)  0.7 us

profile of v1, /device:TPU:26, one launch (start us, length us, event | category | flops | bytes accessed | tf_op | source)
XLA Modules:
  0.0 29.7 jit_solution(15608295139033365085)
XLA Ops:
  0.0 0.0 copy-start.4
  0.7 0.7 %reshape.6.q_gain = f32[1,1280]{1,0:T(1,128)S(1)} reshape(f32[1280]{0:T(1024)} %param.10) | data formatting | bytes 10240 | tf_op jit(solution)/shard_map/reshape | solution.py:322
  1.4 0.0 copy-done.4
  1.4 0.0 copy-start.3
  1.4 0.6 %copy-done.3 = s32[1,2]{1,0:T(1,128)S(1)} copy-done((s32[1,2]{1,0:T(1,128)S(1)}, s32[1,2]{1,0:T(1,128)}, u32[]{:S(2)}) %copy-start.3) | copy-done | bytes 32
  2.0 0.0 copy-start
  2.0 0.9 %copy-done = bf16[96,1280]{1,0:T(8,128)(2,1)S(1)} copy-done((bf16[96,1280]{1,0:T(8,128)(2,1)S(1)}, bf16[96,1280]{1,0:T(8,128)(2,1)}, u32[]{:S(2)}) %copy-start) | copy-done | bytes 245784
  3.0 0.0 copy-start.1
  3.0 0.9 %copy-done.1 = bf16[96,1280]{1,0:T(8,128)(2,1)S(1)} copy-done((bf16[96,1280]{1,0:T(8,128)(2,1)S(1)}, bf16[96,1280]{1,0:T(8,128)(2,1)}, u32[]{:S(2)}) %copy-start.1) | copy-done | bytes 245784
  3.9 0.0 copy-start.2
  3.9 0.9 %copy-done.2 = bf16[96,1280]{1,0:T(8,128)(2,1)S(1)} copy-done((bf16[96,1280]{1,0:T(8,128)(2,1)S(1)}, bf16[96,1280]{1,0:T(8,128)(2,1)}, u32[]{:S(2)}) %copy-start.2) | copy-done | bytes 245784
  4.9 24.2 %shard_map.73 = bf16[96,1280]{1,0:T(8,128)(2,1)S(1)} custom-call(bf16[96,1280]{1,0:T(8,128)(2,1)S(1)} %copy-done, bf16[96,1280]{1,0:T(8,128)(2,1)S(1)} %copy-done.1, bf16[96,1280]{1,0:T(8,128)(2,1)S(1)} %copy-done.2, f32[1,1280]{1,0:T(1,128)S(1)} %reshape.6.q_gain, f32[1,1280]{1,0:T(1,128)S(1)} %reshape.7.k_gain, s32[1]{0:T(128)S(6)} %copy.9.frames, ...), custom_call_target="tpu_custom_call" | custom-call | tf_op jit(solution)/shard_map/pallas_call | solution.py:293
  29.0 0.7 %copy.10 = bf16[96,1280]{1,0:T(8,128)(2,1)} copy(bf16[96,1280]{1,0:T(8,128)(2,1)S(1)} %shard_map.73) | data formatting | bytes 491520
  (1 shorter events, 0.0 us)
Async XLA Ops:
  0.0 1.4 %copy-start.4 = (f32[1280]{0:T(1024)S(1)}, f32[1280]{0:T(1024)}, u32[]{:S(2)}) copy-start(f32[1280]{0:T(1024)} %param.11) | copy-start | bytes 15364
  1.4 0.7 %copy-start.3 = (s32[1,2]{1,0:T(1,128)S(1)}, s32[1,2]{1,0:T(1,128)}, u32[]{:S(2)}) copy-start(s32[1,2]{1,0:T(1,128)} %flags.1) | copy-start | bytes 28
  2.0 0.9 %copy-start = (bf16[96,1280]{1,0:T(8,128)(2,1)S(1)}, bf16[96,1280]{1,0:T(8,128)(2,1)}, u32[]{:S(2)}) copy-start(bf16[96,1280]{1,0:T(8,128)(2,1)} %q_hbm.1) | copy-start | bytes 737284
  3.0 0.9 %copy-start.1 = (bf16[96,1280]{1,0:T(8,128)(2,1)S(1)}, bf16[96,1280]{1,0:T(8,128)(2,1)}, u32[]{:S(2)}) copy-start(bf16[96,1280]{1,0:T(8,128)(2,1)} %k_hbm.1) | copy-start | bytes 737284
  3.9 0.9 %copy-start.2 = (bf16[96,1280]{1,0:T(8,128)(2,1)S(1)}, bf16[96,1280]{1,0:T(8,128)(2,1)}, u32[]{:S(2)}) copy-start(bf16[96,1280]{1,0:T(8,128)(2,1)} %v_hbm.1) | copy-start | bytes 737284

commit v2 on v1

v2 whole, which is shorter than its diff:
```python
import functools
import math

import jax
import jax.numpy as jnp
from jax import lax
from jax.experimental import pallas as pl
from jax.experimental.pallas import tpu as pltpu
from jax.sharding import PartitionSpec as P

HD = 128
FT = 32
EPSILON = 1e-06
MASKED = -1e30

PIECES = 2
CROSSING = (0, 1, 2, 3)
K_ENERGY, Q_ENERGY, COUNT, V_NEW, K_NEW, V_OLD, K_OLD, V_SINK = range(8)
K_SINK = V_SINK + PIECES
COPIES = K_SINK + PIECES


def kernel(spans, heads_axis, q_hbm, k_hbm, v_hbm, q_gain_hbm, k_gain_hbm, frames_hbm, flags_hbm, out,
           q_gain, k_gain, frames, flags, q_raw, k_raw, q_norm, k_all, v_all, energy, energy_in, count, count_in,
           v_new, k_new, v_old, k_old, own_max, own_sum, own_out,
           local_sem, send_sem, recv_sem, hop_sem):
    rows, cols = q_hbm.shape
    heads = cols // HD
    window = 2 * FT
    older, newer, sink = rows, rows + FT, rows + window
    full_width = cols * heads_axis
    t = lax.axis_index("tm")
    even = t % 2 == 0
    side = lax.axis_index("head")

    def column(h):
        return pl.ds(h * HD, HD)

    def load(source, target, index):
        return pltpu.make_async_copy(source, target, local_sem.at[index])

    loads = [load(k_hbm, k_raw, 0), load(v_hbm, v_all.at[pl.ds(0, rows)], 1),
             load(frames_hbm, frames, 2), load(flags_hbm, flags, 3), load(k_gain_hbm, k_gain, 4),
             load(q_hbm, q_raw, 5), load(q_gain_hbm, q_gain, 6)]
    for copy in loads:
        copy.start()

    barrier = pltpu.get_barrier_semaphore()

    def greet(condition, **where):
        @pl.when(condition)
        def _():
            pl.semaphore_signal(barrier, inc=1, device_id=where, device_id_type=pl.DeviceIdType.MESH)

    for other in range(1, heads_axis):
        greet(side >= 0, head=lax.rem(side + other, heads_axis))
    partners = heads_axis - 1
    for step in (-2, -1, 1, 2):
        there = (t + step >= 0) & (t + step < spans)
        greet(there, tm=t + step)
        partners = partners + there.astype(jnp.int32)

    @pl.when(t == 0)
    def _():
        blank = jnp.zeros((window, cols), jnp.bfloat16)
        k_all[pl.ds(older, window)] = blank
        v_all[pl.ds(older, window)] = blank
        count_in[...] = jnp.zeros_like(count_in)

    def remote(kind, source, target, sem=None, **where):
        return pltpu.make_async_remote_copy(
            src_ref=source, dst_ref=target,
            send_sem=send_sem.at[kind] if sem is None else sem, recv_sem=recv_sem.at[kind],
            device_id=where, device_id_type=pl.DeviceIdType.MESH)

    after = {"tm": jnp.minimum(t + 1, spans - 1)}
    hop = {"tm": jnp.minimum(t + 2, spans - 1)}
    has_after = t + 1 < spans
    has_hop = t + 2 < spans

    def squares(ref):
        total = jnp.zeros((rows, HD), jnp.float32)
        for h in range(heads):
            block = ref[:, column(h)].astype(jnp.float32)
            total = total + block * block
        return total

    def piece(i):
        first, last = heads * i // PIECES, heads * (i + 1) // PIECES
        return pl.ds(first * HD, (last - first) * HD)

    def sink_sends(kind, ref, i):
        at = ref.at[pl.ds(sink, FT), piece(i)]
        index = kind - V_SINK + i
        along = remote(kind + i, at, at, sem=hop_sem.at[index], **hop)
        across = remote(kind + i, at, at, **after)
        return along, across

    def sink_goes(kind, i):
        if kind - V_SINK + i in CROSSING:
            return even & has_hop, even & has_after
        return has_hop, (t == 0) & has_after

    def sink_pass(kind, ref, i):
        along, across = sink_sends(kind, ref, i)
        goes_along, goes_across = sink_goes(kind, i)

        @pl.when(goes_along)
        def _():
            along.start()

        @pl.when(goes_across)
        def _():
            across.start()

    def sink_take(kind, ref, i):
        @pl.when(t > 0)
        def _():
            sink_sends(kind, ref, i)[1].wait_recv()
            sink_pass(kind, ref, i)

    def newest(source, target):
        for h in range(heads):
            a, b, c = (source[pl.ds(i * FT, FT), column(h)] for i in range(3))
            target[:, column(h)] = jnp.where(n >= 3 * FT, c, jnp.where(n >= 2 * FT, b, a))

    def second(source, target):
        for h in range(heads):
            a, b = (source[pl.ds(i * FT, FT), column(h)] for i in range(2))
            got = source[pl.ds(newer, FT), column(h)]
            target[:, column(h)] = jnp.where(n >= 3 * FT, b, jnp.where(n >= 2 * FT, a, got))

    counts = remote(COUNT, count, count_in, **after)
    sends = {
        V_NEW: remote(V_NEW, v_new, v_all.at[pl.ds(newer, FT)], **after),
        K_NEW: remote(K_NEW, k_new, k_all.at[pl.ds(newer, FT)], **after),
        V_OLD: remote(V_OLD, v_old, v_all.at[pl.ds(older, FT)], **after),
        K_OLD: remote(K_OLD, k_old, k_all.at[pl.ds(older, FT)], **after),
    }
    shares = [remote(kind, energy.at[kind], energy_in.at[kind], head=lax.rem(side + 1, heads_axis))
              for kind in (K_ENERGY, Q_ENERGY)]

    for copy in loads[:5]:
        copy.wait()
    n = frames[0] * FT
    count[...] = jnp.full(count.shape, n, jnp.int32)
    energy[K_ENERGY] = squares(k_raw)
    newest(v_all, v_new)

    @pl.when(t == 0)
    def _():
        v_all[pl.ds(sink, FT)] = v_all[pl.ds(0, FT)]

    pl.semaphore_wait(barrier, partners)
    shares[K_ENERGY].start()

    @pl.when(t == 0)
    def _():
        for i in range(PIECES):
            sink_pass(V_SINK, v_all, i)

    @pl.when(has_after)
    def _():
        sends[V_NEW].start()
        counts.start()

    for copy in loads[5:]:
        copy.wait()
    energy[Q_ENERGY] = squares(q_raw)
    shares[Q_ENERGY].start()

    def level(index):
        shares[index].wait()
        total = jnp.sum(energy[index] + energy_in[index], axis=1, keepdims=True)
        return lax.rsqrt(total / full_width + EPSILON)

    k_level = level(K_ENERGY)
    for h in range(heads):
        k_all[pl.ds(0, rows), column(h)] = (
            k_raw[:, column(h)].astype(jnp.float32) * k_level * k_gain[column(h)].reshape(1, HD)
        ).astype(jnp.bfloat16)

    @pl.when(t == 0)
    def _():
        k_all[pl.ds(sink, FT)] = k_all[pl.ds(0, FT)]
        for i in range(PIECES):
            sink_pass(K_SINK, k_all, i)

    newest(k_all, k_new)

    @pl.when(has_after)
    def _():
        sends[K_NEW].start()

    q_level = level(Q_ENERGY)
    for h in range(heads):
        q_norm[:, column(h)] = (
            q_raw[:, column(h)].astype(jnp.float32) * q_level * q_gain[column(h)].reshape(1, HD)
        ).astype(jnp.bfloat16)

    def received(kind):
        @pl.when(t > 0)
        def _():
            sends[kind].wait_recv()

    scaling = math.log2(math.e) / math.sqrt(HD)

    def scores(h, start, allowed):
        products = lax.dot_general(
            q_norm[:, column(h)], k_all[pl.ds(start, rows), column(h)],
            (((1,), (1,)), ((), ())), preferred_element_type=jnp.float32)
        return jnp.where(allowed, products * scaling, MASKED)

    def mix(weight, h, start):
        return jnp.dot(weight, v_all[pl.ds(start, rows), column(h)],
                       preferred_element_type=jnp.float32)

    ones = jnp.ones((rows, HD), jnp.bfloat16)

    def total_of(weight):
        return jnp.dot(weight, ones, preferred_element_type=jnp.float32)

    lane = lax.broadcasted_iota(jnp.int32, (1, rows), 1)
    live_keys = lane < n
    live_rows = lax.broadcasted_iota(jnp.int32, (rows, 1), 0) < n

    def own(h):
        s = scores(h, 0, live_keys)
        top = jnp.max(s, axis=1, keepdims=True)
        weight = jnp.exp2(s - top)
        own_max[h] = top
        weight = weight.astype(jnp.bfloat16)
        own_sum[:, column(h)] = total_of(weight)
        own_out[:, column(h)] = mix(weight, h, 0)

    received(V_NEW)
    second(v_all, v_old)

    @pl.when(has_after)
    def _():
        sends[V_OLD].start()

    received(K_NEW)
    second(k_all, k_old)

    @pl.when(has_after)
    def _():
        sends[K_OLD].start()

    stages = 2 * PIECES
    for stage in range(stages):
        if stage < PIECES:
            sink_take(V_SINK, v_all, stage)
        else:
            sink_take(K_SINK, k_all, stage - PIECES)
        for h in range(heads * stage // stages, heads * (stage + 1) // stages):
            own(h)

    @pl.when(t > 0)
    def _():
        counts.wait_recv()

    received(V_OLD)
    received(K_OLD)

    use_sink = flags[0, 0]
    use_window = flags[0, 1]
    held = jnp.where(t >= 2, window, count_in[0:1, :rows])
    allowed = jnp.where(
        lane >= window, use_sink,
        use_window * jnp.where(lane >= FT, (held > 0).astype(jnp.int32),
                               (held >= window).astype(jnp.int32))) > 0

    for h in range(heads):
        s = scores(h, older, allowed)
        top = jnp.maximum(jnp.max(s, axis=1, keepdims=True), own_max[h])
        weight = jnp.exp2(s - top).astype(jnp.bfloat16)
        keep = jnp.exp2(own_max[h] - top)
        denominator = total_of(weight) + own_sum[:, column(h)] * keep
        total = mix(weight, h, older) + own_out[:, column(h)] * keep
        out[:, column(h)] = jnp.where(live_rows, total / denominator, 0.0).astype(jnp.bfloat16)

    @pl.when(has_after)
    def _():
        counts.wait_send()
        for copy in sends.values():
            copy.wait_send()

    for kind, ref in ((V_SINK, v_all), (K_SINK, k_all)):
        for i in range(PIECES):
            along, across = sink_sends(kind, ref, i)
            goes_along, goes_across = sink_goes(kind, i)

            @pl.when(goes_along)
            def _():
                along.wait_send()

            @pl.when(goes_across)
            def _():
                across.wait_send()


def local(spans, heads_axis, queries, keys, values, q_gain, k_gain, frames, flags):
    rows, cols = queries.shape
    heads = cols // HD
    far = pl.BlockSpec(memory_space=pltpu.HBM)
    near = pl.BlockSpec(memory_space=pltpu.VMEM)
    bf16, f32 = jnp.bfloat16, jnp.float32
    held = 2 * rows
    return pl.pallas_call(
        functools.partial(kernel, spans, heads_axis),
        out_shape=pltpu.VMEM((rows, cols), bf16),
        in_specs=[far] * 7,
        out_specs=near,
        scratch_shapes=[
            pltpu.VMEM((cols,), f32),
            pltpu.VMEM((cols,), f32),
            pltpu.SMEM(frames.shape, jnp.int32),
            pltpu.SMEM(flags.shape, jnp.int32),
            pltpu.VMEM((rows, cols), bf16),
            pltpu.VMEM((rows, cols), bf16),
            pltpu.VMEM((rows, cols), bf16),
            pltpu.VMEM((held, cols), bf16),
            pltpu.VMEM((held, cols), bf16),
            pltpu.VMEM((2, rows, HD), f32),
            pltpu.VMEM((2, rows, HD), f32),
            pltpu.VMEM((8, HD), jnp.int32),
            pltpu.VMEM((8, HD), jnp.int32),
            pltpu.VMEM((FT, cols), bf16),
            pltpu.VMEM((FT, cols), bf16),
            pltpu.VMEM((FT, cols), bf16),
            pltpu.VMEM((FT, cols), bf16),
            pltpu.VMEM((heads, rows, 1), f32),
            pltpu.VMEM((rows, cols), f32),
            pltpu.VMEM((rows, cols), f32),
            pltpu.SemaphoreType.DMA((7,)),
            pltpu.SemaphoreType.DMA((COPIES,)),
            pltpu.SemaphoreType.DMA((COPIES,)),
            pltpu.SemaphoreType.DMA((2 * PIECES,)),
        ],
        compiler_params=pltpu.CompilerParams(
            collective_id=0, has_side_effects=True, vmem_limit_bytes=63 * 2**20),
    )(queries, keys, values, q_gain, k_gain, frames, flags)


def solution(mesh):
    placed = (
        P(("groups", "tm"), "head"),
        P(("groups", "tm"), "head"),
        P(("groups", "tm"), "head"),
        P("head"),
        P("head"),
        P(("groups", "tm")),
        P(("groups", "tm"), None),
    )
    return jax.shard_map(
        functools.partial(local, mesh.shape["tm"], mesh.shape["head"]),
        mesh=mesh, in_specs=placed, out_specs=P(("groups", "tm"), "head"), check_vma=False
    )
```

time: 30 us -> 20.2 us (0.67)
  Pallas kernels: 24.2 us -> 18.7 us
  local copies, waits for them, and re-layouts: 4.88 us -> 0.7 us
    pallas_call x1, Pallas kernels: 24.2 us -> 18.7 us  [local(): pl.pallas_call(functools.partial(kernel, spans, heads_axis), out_shape=pl...]
    unnamed x11 -> x1, local copies, waits for them, and re-layouts: 4.17 us -> 0.7 us
    reshape x2 -> x0, local copies, waits for them, and re-layouts: 0.71 us -> none  [the longest x1 0.7 us: local(): q_gain.reshape(1, cols)]
where the time goes in v2:
time: 20.2 us; the launch traced here: 20 us
  Pallas kernels  18.7 us (93%)
  local copies, waits for them, and re-layouts  0.7 us (3%)
  between operations  0.66 us (3%)
    pallas_call x1, Pallas kernels, local(): pl.pallas_call(functools.partial(kernel, spans, heads_axis), out_shape=pl...  18.7 us
    unnamed x1, local copies, waits for them, and re-layouts  0.7 us

profile of v2, /device:TPU:26, one launch (start us, length us, event | category | flops | bytes accessed | tf_op | source)
XLA Modules:
  0.0 20.0 jit_solution(18063105215478550288)
XLA Ops:
  0.7 18.7 %shard_map.73 = bf16[96,1280]{1,0:T(8,128)(2,1)S(1)} custom-call(bf16[96,1280]{1,0:T(8,128)(2,1)} %q_hbm.1, bf16[96,1280]{1,0:T(8,128)(2,1)} %k_hbm.1, bf16[96,1280]{1,0:T(8,128)(2,1)} %v_hbm.1, f32[1280]{0:T(1024)} %q_gain_hbm.1, f32[1280]{0:T(1024)} %k_gain_hbm.1, s32[1]{0:T(128)S(6)} %copy.10.frames_hbm, s32[1,2]{1,0:T(1,128)} %flags_hbm.1), custom_call_target="tpu_custom_call" | custom-call | tf_op jit(solution)/shard_map/pallas_call | solution.py:310
  19.3 0.7 %copy.9 = bf16[96,1280]{1,0:T(8,128)(2,1)} copy(bf16[96,1280]{1,0:T(8,128)(2,1)S(1)} %shard_map.73) | data formatting | bytes 491520

commit v3 on v2

--- a/solution.py
+++ b/solution.py
@@ -233,28 +233,44 @@
         own_sum[:, column(h)] = total_of(weight)
         own_out[:, column(h)] = mix(weight, h, 0)
 
-    received(V_NEW)
-    second(v_all, v_old)
-
-    @pl.when(has_after)
-    def _():
-        sends[V_OLD].start()
-
-    received(K_NEW)
-    second(k_all, k_old)
-
-    @pl.when(has_after)
-    def _():
-        sends[K_OLD].start()
-
-    stages = 2 * PIECES
-    for stage in range(stages):
-        if stage < PIECES:
-            sink_take(V_SINK, v_all, stage)
-        else:
-            sink_take(K_SINK, k_all, stage - PIECES)
-        for h in range(heads * stage // stages, heads * (stage + 1) // stages):
-            own(h)
+    def hand_on(new, old, ref, scratch):
+        received(new)
+        second(ref, scratch)
+
+        @pl.when(has_after)
+        def _():
+            sends[old].start()
+
+    def follow(order):
+        done = 0
+        for step, (what, ready) in enumerate(order):
+            if what == V_NEW:
+                hand_on(V_NEW, V_OLD, v_all, v_old)
+            elif what == K_NEW:
+                hand_on(K_NEW, K_OLD, k_all, k_old)
+            elif what < K_SINK:
+                sink_take(V_SINK, v_all, what - V_SINK)
+            else:
+                sink_take(K_SINK, k_all, what - K_SINK)
+            for h in range(done, ready):
+                own(h)
+            done = ready
+        assert done == heads
+
+    def spaced(order, counts):
+        total = sum(counts)
+        return [(what, heads * sum(counts[:i + 1]) // total) for i, what in enumerate(order)]
+
+    v_sinks = [V_SINK + i for i in range(PIECES)]
+    k_sinks = [K_SINK + i for i in range(PIECES)]
+
+    @pl.when(even)
+    def _():
+        follow(spaced(v_sinks + [V_NEW, K_NEW] + k_sinks, [0, 1, 1, 3, 3, 2]))
+
+    @pl.when(jnp.logical_not(even))
+    def _():
+        follow(spaced([V_NEW, K_NEW] + v_sinks + k_sinks, [3, 2, 2, 1, 1, 1]))
 
     @pl.when(t > 0)
     def _():

time: 20.2 us -> 18.9 us (0.936)
  Pallas kernels: 18.7 us -> 17.4 us
    pallas_call x1, Pallas kernels: 18.7 us -> 17.4 us  [local(): pl.pallas_call(functools.partial(kernel, spans, heads_axis), out_shape=pl...]
where the time goes in v3:
time: 18.9 us; the launch traced here: 18.7 us
  Pallas kernels  17.4 us (92%)
  local copies, waits for them, and re-layouts  0.7 us (4%)
  between operations  0.66 us (3%)
    pallas_call x1, Pallas kernels, local(): pl.pallas_call(functools.partial(kernel, spans, heads_axis), out_shape=pl...  17.4 us
    unnamed x1, local copies, waits for them, and re-layouts  0.7 us

profile of v3, /device:TPU:26, one launch (start us, length us, event | category | flops | bytes accessed | tf_op | source)
XLA Modules:
  0.0 18.7 jit_solution(10897474836680520206)
XLA Ops:
  0.7 17.4 %shard_map.73 = bf16[96,1280]{1,0:T(8,128)(2,1)S(1)} custom-call(bf16[96,1280]{1,0:T(8,128)(2,1)} %q_hbm.1, bf16[96,1280]{1,0:T(8,128)(2,1)} %k_hbm.1, bf16[96,1280]{1,0:T(8,128)(2,1)} %v_hbm.1, f32[1280]{0:T(1024)} %q_gain_hbm.1, f32[1280]{0:T(1024)} %k_gain_hbm.1, s32[1]{0:T(128)S(6)} %copy.10.frames_hbm, s32[1,2]{1,0:T(1,128)} %flags_hbm.1), custom_call_target="tpu_custom_call" | custom-call | tf_op jit(solution)/shard_map/pallas_call | solution.py:326
  18.0 0.7 %copy.9 = bf16[96,1280]{1,0:T(8,128)(2,1)} copy(bf16[96,1280]{1,0:T(8,128)(2,1)S(1)} %shard_map.73) | data formatting | bytes 491520

commit v4 on v3

--- a/solution.py
+++ b/solution.py
@@ -13,8 +13,8 @@
 EPSILON = 1e-06
 MASKED = -1e30
 
-PIECES = 2
-CROSSING = (0, 1, 2, 3)
+PIECES = 3
+CROSSING = tuple(range(6))
 K_ENERGY, Q_ENERGY, COUNT, V_NEW, K_NEW, V_OLD, K_OLD, V_SINK = range(8)
 K_SINK = V_SINK + PIECES
 COPIES = K_SINK + PIECES
@@ -266,11 +266,11 @@
 
     @pl.when(even)
     def _():
-        follow(spaced(v_sinks + [V_NEW, K_NEW] + k_sinks, [0, 1, 1, 3, 3, 2]))
+        follow(spaced(v_sinks + [V_NEW, K_NEW] + k_sinks, [0, 0, 1, 1, 3, 2, 2, 1]))
 
     @pl.when(jnp.logical_not(even))
     def _():
-        follow(spaced([V_NEW, K_NEW] + v_sinks + k_sinks, [3, 2, 2, 1, 1, 1]))
+        follow(spaced([V_NEW, K_NEW] + v_sinks + k_sinks, [3, 2, 1, 1, 1, 1, 1, 0]))
 
     @pl.when(t > 0)
     def _():

time: 18.9 us -> 18.7 us (0.989)
  Pallas kernels: 17.4 us -> 17.2 us
where the time goes in v4:
time: 18.7 us; the launch traced here: 18.6 us
  Pallas kernels  17.2 us (92%)
  local copies, waits for them, and re-layouts  0.7 us (4%)
  between operations  0.66 us (4%)
    pallas_call x1, Pallas kernels, local(): pl.pallas_call(functools.partial(kernel, spans, heads_axis), out_shape=pl...  17.2 us
    unnamed x1, local copies, waits for them, and re-layouts  0.7 us

profile of v4, /device:TPU:26, one launch (start us, length us, event | category | flops | bytes accessed | tf_op | source)
XLA Modules:
  0.0 18.6 jit_solution(1914483781716620688)
XLA Ops:
  0.7 17.2 %shard_map.73 = bf16[96,1280]{1,0:T(8,128)(2,1)S(1)} custom-call(bf16[96,1280]{1,0:T(8,128)(2,1)} %q_hbm.1, bf16[96,1280]{1,0:T(8,128)(2,1)} %k_hbm.1, bf16[96,1280]{1,0:T(8,128)(2,1)} %v_hbm.1, f32[1280]{0:T(1024)} %q_gain_hbm.1, f32[1280]{0:T(1024)} %k_gain_hbm.1, s32[1]{0:T(128)S(6)} %copy.10.frames_hbm, s32[1,2]{1,0:T(1,128)} %flags_hbm.1), custom_call_target="tpu_custom_call" | custom-call | tf_op jit(solution)/shard_map/pallas_call | solution.py:326
  17.9 0.7 %copy.9 = bf16[96,1280]{1,0:T(8,128)(2,1)} copy(bf16[96,1280]{1,0:T(8,128)(2,1)S(1)} %shard_map.73) | data formatting | bytes 491520
